TPU v7x, 32 devices: a whole 2x2x4 slice. The times are simulated.
32 devices in a mesh: req: 16 (over z, y, x), tp: 2 (over core).
Axes of the slice: x: 2, y: 2, z: 4, core: 2. Of those that a mesh axis runs over, the one named last changes fastest.
Arguments:
- q_proj: bfloat16 [16, 128, 768], P('req', None, 'tp'), may hold values from -24 to 24, as said below
- kv_proj: bfloat16 [16, 128, 2, 256], P('req', None, None, 'tp'), may hold values from -6 to 6
- q_bias: bfloat16 [768], P('tp'), may hold values from -3 to 3
- kv_bias: bfloat16 [2, 256], P(None, 'tp'), may hold values from -3 to 3
- prefix_kv: bfloat16 [16, 1024, 2, 256], P('req', None, None, 'tp'), may hold values from -24 to 24, as said below
- lengths: int32 [16], P('req'), may hold values from 1 to 128, 1024 in all
- group_of: int32 [16], P('req'), may hold values from 0 to 2
- owner: int32 [3], replicated, may hold values from 0 to 15
- positions: int32 [16, 128], P('req'), may hold values from 1024 to 1278, as said below
- residual: bfloat16 [16, 128, 5120], P('req', None, 'tp'), may hold values from -6 to 6
- out_weight: bfloat16 [768, 5120], P(None, 'tp'), may hold values from -0.21875 to 0.21875
Outputs:
- hidden: bfloat16 [16, 128, 5120], P('req', None, 'tp')
Inputs may be any that keep to these rules, and one draw needn't show every extreme that they name: `q_proj`: projected queries; entries stay within the stated bounds. `prefix_kv`: cached keys are already rotated at prefix positions 0 to 1023. Each request's positions are a start of 1024 or more plus the slot index.
All inputs are finite; a program needn't handle non-finite values. No bound on the sum of `lengths` on one device may be relied on, other than what follows from the above.
Results may differ from a plain program's by a relative error of at most 0.006.
Values may be sent and summed in bfloat16 or wider, within the bound.
A program may use at most 128 MiB of HBM per device.

v0:
```python
import math

import jax
import jax.numpy as jnp
from jax import lax
from jax.sharding import PartitionSpec as P

HD = 128


def spread(x, axis, root):
    mine = lax.axis_index(axis) == root
    return lax.psum(jnp.where(mine, x, jnp.zeros_like(x)), axis)


def rotate(vectors, places):
    half = HD // 2
    index = jnp.arange(half).astype(jnp.float32)
    freqs = jnp.exp(index * (-2.0 / HD) * math.log(1000000.0))
    angles = places.astype(jnp.float32)[:, None] * freqs[None, :]
    cosine = jnp.concatenate([jnp.cos(angles), jnp.cos(angles)], axis=-1)[:, None, :]
    sine = jnp.concatenate([jnp.sin(angles), jnp.sin(angles)], axis=-1)[:, None, :]
    turned = jnp.concatenate([-vectors[..., half:], vectors[..., :half]], axis=-1)
    return vectors * cosine + turned * sine


def attend_rows(queries, all_keys, all_vals, length, prefix_len):
    count = queries.shape[0]
    slots = jnp.arange(count)
    causal = slots[None, :] <= slots[:, None]
    allowed = jnp.concatenate([jnp.ones((count, prefix_len), dtype=bool), causal], axis=1)
    scores = jnp.einsum("rhd,kd->hrk", queries, all_keys, preferred_element_type=jnp.float32) * (
        1.0 / math.sqrt(HD)
    )
    scores = jnp.where(allowed[None], scores, -1e30)
    top = jnp.max(scores, axis=-1, keepdims=True)
    weights = jnp.where(allowed[None], jnp.exp(scores - top), 0.0)
    total = jnp.sum(weights, axis=-1)
    rounded = weights.astype(jnp.bfloat16)
    mixed = jnp.einsum("hrk,kd->rhd", rounded, all_vals, preferred_element_type=jnp.float32)
    mixed = mixed / jnp.transpose(total)[:, :, None]
    mixed = jnp.where((slots < length)[:, None, None], mixed, 0.0)
    return mixed.astype(jnp.bfloat16)


def body(
    q_proj,
    kv_proj,
    q_bias,
    kv_bias,
    prefix_kv,
    lengths,
    group_of,
    owner,
    positions,
    residual,
    out_weight,
):
    cap = q_proj.shape[1]
    prefix_len = prefix_kv.shape[1]
    mine = group_of[0]
    length = lengths[0]
    places = positions[0]
    queries = q_proj[0].astype(jnp.float32).reshape(cap, -1, HD) + q_bias.astype(
        jnp.float32
    ).reshape(-1, HD)
    queries = rotate(queries, places).astype(jnp.bfloat16)
    pairs = kv_proj[0].astype(jnp.float32) + kv_bias.astype(jnp.float32)
    keys = rotate(pairs[:, 0][:, None, :], places)[:, 0].astype(jnp.bfloat16)
    vals = pairs[:, 1].astype(jnp.bfloat16)
    slab = jnp.zeros_like(prefix_kv[0])
    for group in range(owner.shape[0]):
        received = spread(prefix_kv[0], "req", owner[group])
        slab = jnp.where(mine == group, received, slab)
    all_keys = jnp.concatenate([slab[:, 0], keys], axis=0)
    all_vals = jnp.concatenate([slab[:, 1], vals], axis=0)
    attended = attend_rows(queries, all_keys, all_vals, length, prefix_len)
    attended = attended.reshape(cap, -1)
    whole_heads = lax.all_gather(attended, "tp", axis=1, tiled=True)
    projected = jnp.dot(whole_heads, out_weight, preferred_element_type=jnp.float32)
    hidden = (residual[0].astype(jnp.float32) + projected).astype(jnp.bfloat16)
    return hidden[None]


def solution(mesh):
    in_specs = (
        P("req", None, "tp"),
        P("req", None, None, "tp"),
        P("tp"),
        P(None, "tp"),
        P("req", None, None, "tp"),
        P("req"),
        P("req"),
        P(),
        P("req", None),
        P("req", None, "tp"),
        P(None, "tp"),
    )
    out_specs = P("req", None, "tp")
    return jax.shard_map(body, mesh=mesh, in_specs=in_specs, out_specs=out_specs, check_vma=False)
```

profile of v0, /device:TPU:1, one launch (start us, length us, event | category | flops | bytes accessed | tf_op | source)
XLA Modules:
  0.0 149.4 jit_solution(16855544040478582796)
XLA Ops:
  6.5 0.0 all-reduce.4.cloned.1.call-start
  6.5 1.4 fusion.31
  9.9 0.0 copy-start.4
  9.9 0.0 copy-start.1
  9.9 2.3 %select_bitcast_fusion = (bf16[1024,2,128]{2,0,1:T(8,128)(2,1)}, bf16[1024,2,128]{2,0,1:T(8,128)(2,1)}, bf16[1024,2,128]{2,0,1:T(8,128)(2,1)}) fusion(pred[]{:T(512)S(6)} %eq.35, bf16[1,1024,2,128]{3,2,1,0:T(2,128)(2,1)} %param.15, pred[]{:T(512)S(6)} %eq.32, pred[]{:T(512)S(6)} %eq.29), kind=kLoop, calls=%fused_computation.16 | loop fusion | flops 786432 | bytes 2097155 | tf_op jit(solution)/shard_map/jit(_where)/select_n | solution.py:13
  12.2 0.0 copy-start.5
  12.2 0.0 copy-start.2
  12.2 0.0 copy-start.3
  12.2 0.0 all-reduce.4.cloned.1.call-update
  12.9 0.0 copy-done.4
  12.9 0.3 fusion.22
  13.3 0.1 pad_maximum_fusion
  13.4 0.1 copy.24
  13.5 0.1 copy.25
  13.6 0.0 copy-done.1
  13.6 0.1 copy.23
  13.7 0.0 copy-done.5
  14.4 0.0 copy-done.2
  14.5 0.0 copy-done.3
  14.5 0.1 slice_negate_fusion.1
  14.6 0.1 fusion.21
  14.7 0.1 convert_add_fusion
  14.9 0.1 fusion.17
  15.0 118.7 %all-reduce.4.cloned.1.call-done = (bf16[1024,2,128]{2,0,1:T(8,128)(2,1)}, bf16[1024,2,128]{2,0,1:T(8,128)(2,1)}, bf16[1024,2,128]{2,0,1:T(8,128)(2,1)}) async-done(((bf16[1024,2,128]{2,0,1:T(8,128)(2,1)}, bf16[1024,2,128]{2,0,1:T(8,128)(2,1)}, bf16[1024,2,128]{2,0,1:T(8,128)(2,1)}), (bf16[1024,2,128]{2,0,1:T(8,128)(2,1)}, bf16[1024,2,128]{2,0,1:T(8,128)(2,1)}, ...) | async-done | bytes 1572880 | tf_op jit(solution)/shard_map/psum | solution.py:13
  133.7 1.1 select_select_fusion
  134.8 0.9 fusion.32
  135.8 0.4 fusion.5
  136.2 0.0 copy-start
  136.2 0.6 fusion.10
  136.8 2.1 %all_gather.3 = bf16[128,768]{0,1:T(8,128)(2,1)S(1)} all-gather(bf16[128,384]{0,1:T(8,128)(2,1)S(1)} %bitcast.78), channel_id=1, replica_groups=mesh['req'=16,'tp'=2] {'tp'}, dimensions={1}, use_global_device_ids=true | all-gather | bytes 294912 | tf_op jit(solution)/shard_map/all_gather | solution.py:79
  138.8 0.0 copy-done
  138.8 3.7 %fusion.2 = bf16[1,128,2560]{2,1,0:T(8,128)(2,1)} fusion(bf16[128,768]{0,1:T(8,128)(2,1)S(1)} %all_gather.3, bf16[768,2560]{1,0:T(8,128)(2,1)} %param.21, bf16[1,128,2560]{2,1,0:T(8,128)(2,1)S(1)} %copy-done), kind=kOutput, calls=%fused_computation.3 | convolution fusion | flops 504299520 | bytes 5439488 | tf_op jit(solution)/shard_map/dot_general | solution.py:80
  (11 shorter events, 0.2 us)
Async XLA Ops:
  6.5 127.1 %all-reduce.4.cloned.1.call-start = ((), (), s32[]{:S(2)}) async-start(), calls=%async_computation | async-start | bytes 3145728 | tf_op jit(solution)/shard_map/psum | solution.py:13
  9.9 3.1 %copy-start.4 = (s32[1,128]{1,0:T(1,128)S(1)}, s32[1,128]{1,0:T(1,128)}, u32[]{:S(2)}) copy-start(s32[1,128]{1,0:T(1,128)} %param.19) | copy-start | bytes 1540
  9.9 3.7 %copy-start.1 = (bf16[1,128,384]{2,1,0:T(8,128)(2,1)S(1)}, bf16[1,128,384]{2,1,0:T(8,128)(2,1)}, u32[]{:S(2)}) copy-start(bf16[1,128,384]{2,1,0:T(8,128)(2,1)} %param.11) | copy-start | bytes 294916
  12.2 1.5 %copy-start.5 = (bf16[2,128]{1,0:T(2,128)(2,1)S(1)}, bf16[2,128]{1,0:T(2,128)(2,1)}, u32[]{:S(2)}) copy-start(bf16[2,128]{1,0:T(2,128)(2,1)} %param.14) | copy-start | bytes 1540
  12.2 2.2 %copy-start.2 = (bf16[1,128,2,128]{3,2,1,0:T(2,128)(2,1)S(1)}, bf16[1,128,2,128]{3,2,1,0:T(2,128)(2,1)}, u32[]{:S(2)}) copy-start(bf16[1,128,2,128]{3,2,1,0:T(2,128)(2,1)} %param.12) | copy-start | bytes 196612
  12.2 2.3 %copy-start.3 = (bf16[384]{0:T(512)(128)(2,1)S(1)}, bf16[384]{0:T(512)(128)(2,1)}, u32[]{:S(2)}) copy-start(bf16[384]{0:T(512)(128)(2,1)} %param.13) | copy-start | bytes 2308
  136.2 2.7 %copy-start = (bf16[1,128,2560]{2,1,0:T(8,128)(2,1)S(1)}, bf16[1,128,2560]{2,1,0:T(8,128)(2,1)}, u32[]{:S(2)}) copy-start(bf16[1,128,2560]{2,1,0:T(8,128)(2,1)} %param.20) | copy-start | bytes 1966084
Sparse Core Ops, SparseCore 0:
  13.2 120.4 all-reduce.3
where the time goes:
time: 150 us; the launch traced here: 149 us
  waiting for transfers between devices  119 us (79%)
  between operations  16.8 us (11%)
  matrix products  5.56 us (4%)
  other arithmetic  4.34 us (3%)
  blocking collectives  2.07 us (1%)
  local copies, waits for them, and re-layouts  1.84 us (1%)
    psum x1, waiting for transfers between devices, spread(): return lax.psum(jnp.where(mine, x, jnp.zeros_like(x)), axis)  119 us
    dot_general x1, matrix products, body(): jnp.dot(whole_heads, out_weight, preferred_element_type=jnp.float32)  3.66 us
  transfers between devices with their start and end apart: 1, of which 1 were waited for; matrix products, arithmetic and copies ran while one was open for 1% of the time, Pallas kernels for 0%

commit v1 on v0

v1 whole, which is shorter than its diff:
```python
import functools
import math

import jax
import jax.numpy as jnp
from jax import lax
from jax.experimental import pallas as pl
from jax.experimental.pallas import tpu as pltpu
from jax.sharding import PartitionSpec as P

HD = 128
QUAD = 4
PIECES = 4
MESH = pl.DeviceIdType.MESH
BF16 = jnp.bfloat16
F32 = jnp.float32


def kernel(
    n_req,
    n_tp,
    groups,
    length_ref,
    group_ref,
    owner_ref,
    pos_ref,
    q_hbm,
    kv_hbm,
    qb_hbm,
    kvb_hbm,
    slab_hbm,
    res_hbm,
    w_hbm,
    out_ref,
    q_in,
    kv_in,
    qb_in,
    kvb_in,
    res_in,
    w_in,
    queries,
    split,
    gsend,
    grecv,
    gsmem,
    att_all,
    total_ref,
    p1,
    chain,
    fwd,
    outp,
    kvp,
    local_sem,
    p1_send,
    p1_recv,
    ch_send,
    ch_recv,
    p3_send,
    p3_recv,
    g_send,
    g_recv,
    att_send,
    att_recv,
):
    req = lax.axis_index("req")
    tp = lax.axis_index("tp")
    depth = n_req // QUAD
    k = req // QUAD
    q = req % QUAD
    base = k * QUAD
    rows = p1[0].shape[1]
    cap = q_in.shape[0]
    heads = q_in.shape[1] // HD
    feats = q_in.shape[1]

    def mate(d):
        return base + (q + d) % QUAD

    fetches = []
    for i, (src, dst) in enumerate(
        ((q_hbm, q_in), (kv_hbm, kv_in), (qb_hbm, qb_in), (kvb_hbm, kvb_in), (res_hbm, res_in), (w_hbm, w_in))
    ):
        fetches.append(pltpu.make_async_copy(src, dst, local_sem.at[i]))
    for f in fetches[:4]:
        f.start()

    barrier = pltpu.get_barrier_semaphore()
    for d in range(1, QUAD):
        pl.semaphore_signal(barrier, inc=1, device_id=(mate(d), tp), device_id_type=MESH)
    for d in range(1, n_tp):
        pl.semaphore_signal(barrier, inc=1, device_id=(req, (tp + d) % n_tp), device_id_type=MESH)

    @pl.when(k > 0)
    def _():
        pl.semaphore_signal(barrier, inc=1, device_id=(req - QUAD, tp), device_id_type=MESH)

    @pl.when(k < depth - 1)
    def _():
        pl.semaphore_signal(barrier, inc=1, device_id=(req + QUAD, tp), device_id_type=MESH)

    gsend[...] = jnp.full(gsend.shape, group_ref[0], jnp.int32)
    ends = jnp.where(k > 0, 1, 0) + jnp.where(k < depth - 1, 1, 0)
    pl.semaphore_wait(barrier, QUAD - 1 + n_tp - 1 + ends)

    gcopies = []
    for d in range(1, QUAD):
        c = pltpu.make_async_remote_copy(
            src_ref=gsend,
            dst_ref=grecv.at[d - 1],
            send_sem=g_send.at[d - 1],
            recv_sem=g_recv.at[d - 1],
            device_id=(mate(d), tp),
            device_id_type=MESH,
        )
        gcopies.append(c)

    first, own = [], []
    for m in range(PIECES):
        line = []
        for d in range(1, QUAD):
            to = (q + d) % QUAD
            start = pl.multiple_of((to * PIECES + m) * rows, rows)
            c = pltpu.make_async_remote_copy(
                src_ref=slab_hbm.at[pl.ds(start, rows)],
                dst_ref=p1[m].at[q],
                send_sem=p1_send.at[m, d - 1],
                recv_sem=p1_recv.at[m, d - 1],
                device_id=(mate(d), tp),
                device_id_type=MESH,
            )
            c.start()
            line.append(c)
        start = pl.multiple_of((q * PIECES + m) * rows, rows)
        c = pltpu.make_async_copy(slab_hbm.at[pl.ds(start, rows)], p1[m].at[q], local_sem.at[6 + m])
        c.start()
        own.append(c)
        first.append(line)
        if m == 0:
            for g in gcopies:
                g.start()
    for f in fetches[4:]:
        f.start()

    for f in fetches[:4]:
        f.wait()
    lane = lax.broadcasted_iota(jnp.int32, (cap, HD), 1)
    place = (pos_ref[0, 0] + lax.broadcasted_iota(jnp.int32, (cap, HD), 0)).astype(F32)
    index = (lane % (HD // 2)).astype(F32)
    freqs = jnp.exp(index * (-2.0 / HD) * math.log(1000000.0))
    angles = place * freqs
    cosine = jnp.cos(angles)
    sine = jnp.sin(angles)
    sine = jnp.where(lane < HD // 2, -sine, sine)

    def rot(x):
        return x * cosine + pltpu.roll(x, HD // 2, 1) * sine

    for h in range(heads):
        cols = pl.ds(h * HD, HD)
        x = q_in[:, cols].astype(F32) + qb_in[:, cols].astype(F32)
        queries[pl.ds(h * cap, cap), :] = rot(x).astype(BF16)
    split[pl.ds(0, 2 * cap), :] = kv_in[...].astype(F32)
    bias = kvb_in[...].astype(F32)
    keys = rot(split[pl.ds(0, cap, stride=2), :] + bias[0:1, :]).astype(BF16)
    vals = (split[pl.ds(1, cap, stride=2), :] + bias[1:2, :]).astype(BF16)
    scale = 1.0 / math.sqrt(HD)
    nt = (((1,), (1,)), ((), ()))

    qs = queries[...]
    s = lax.dot_general(qs, keys, nt, preferred_element_type=F32) * scale
    seen = lax.broadcasted_iota(jnp.int32, s.shape, 1) <= lax.broadcasted_iota(jnp.int32, s.shape, 0) % cap
    s = jnp.where(seen, s, -1e30)
    top = jnp.max(s, axis=-1, keepdims=True)
    w = jnp.where(seen, jnp.exp(s - top), 0.0)
    tot = jnp.sum(w, axis=-1, keepdims=True)
    acc = jnp.dot(w.astype(BF16), vals, preferred_element_type=F32)

    for d in range(1, QUAD):
        gcopies[d - 1].wait_recv()
    to_smem = pltpu.make_async_copy(grecv, gsmem, local_sem.at[6 + PIECES])
    to_smem.start()
    to_smem.wait()
    wants = [group_ref[0]]
    for d in range(1, QUAD):
        wants.append(gsmem[QUAD - d - 1, 0, 0])

    near = jnp.where(k < depth // 2, 0, 1)

    def chain_copy(m, d):
        step = 1 - 2 * d
        return pltpu.make_async_remote_copy(
            src_ref=fwd[m].at[d],
            dst_ref=chain[m].at[d],
            send_sem=ch_send.at[m, d],
            recv_sem=ch_recv.at[m, d],
            device_id=(req + step * QUAD, tp),
            device_id_type=MESH,
        )

    def has_source(d):
        return jnp.where(d == 0, k, depth - 1 - k) > 0

    def has_target(d):
        return jnp.where(d == 0, depth - 1 - k, k) > 0

    last = []

    def stage_two(m):
        for c in first[m]:
            c.wait_recv()
        own[m].wait()
        for d in (near, 1 - near):

            @pl.when(has_source(d))
            def _():
                chain_copy(m, d).wait_recv()

            @pl.when(has_target(d))
            def _():
                for c in range(groups):
                    o = owner_ref[c]
                    mine = p1[m][o % QUAD]
                    fwd[m][d, c] = jnp.where(o // QUAD == k, mine, chain[m][d, c])
                chain_copy(m, d).start()

        line = []
        for d in (1, 2, 3, 0):
            c = wants[d]
            o = owner_ref[c]
            oz = o // QUAD
            other = jnp.where(oz < k, chain[m][0, c], chain[m][1, c])
            piece = jnp.where(oz == k, p1[m][o % QUAD], other)
            if d == 0:
                kvp[m][q] = piece
            else:
                outp[m][d - 1] = piece
                r = pltpu.make_async_remote_copy(
                    src_ref=outp[m].at[d - 1],
                    dst_ref=kvp[m].at[q],
                    send_sem=p3_send.at[m, d - 1],
                    recv_sem=p3_recv.at[m, d - 1],
                    device_id=(mate(d), tp),
                    device_id_type=MESH,
                )
                r.start()
                line.append(r)
        last.append(line)

    def attend(m, top, tot, acc):
        for r in last[m]:
            r.wait_recv()
        for j in range(QUAD):
            split[pl.ds(j * rows, rows), :] = kvp[m][j].astype(F32)
        half = QUAD * rows // 2
        ks = split[pl.ds(0, half, stride=2), :].astype(BF16)
        vs = split[pl.ds(1, half, stride=2), :].astype(BF16)
        s = lax.dot_general(queries[...], ks, nt, preferred_element_type=F32) * scale
        new = jnp.maximum(top, jnp.max(s, axis=-1, keepdims=True))
        fade = jnp.exp(top - new)
        w = jnp.exp(s - new)
        tot = tot * fade + jnp.sum(w, axis=-1, keepdims=True)
        acc = acc * fade + jnp.dot(w.astype(BF16), vs, preferred_element_type=F32)
        return new, tot, acc

    for m in range(PIECES):
        stage_two(m)
        if m > 0:
            top, tot, acc = attend(m - 1, top, tot, acc)
    top, tot, acc = attend(PIECES - 1, top, tot, acc)

    mixed = acc / tot
    slot = lax.broadcasted_iota(jnp.int32, mixed.shape, 0) % cap
    mixed = jnp.where(slot < length_ref[0], mixed, 0.0).astype(BF16)
    for h in range(heads):
        att_all[tp, :, pl.ds(h * HD, HD)] = mixed[h * cap : (h + 1) * cap, :]
    attc = []
    for d in range(1, n_tp):
        c = pltpu.make_async_remote_copy(
            src_ref=att_all.at[tp],
            dst_ref=att_all.at[tp],
            send_sem=att_send.at[d - 1],
            recv_sem=att_recv.at[d - 1],
            device_id=(req, (tp + d) % n_tp),
            device_id_type=MESH,
        )
        c.start()
        attc.append(c)
    for f in fetches[4:]:
        f.wait()
    width = out_ref.shape[1]
    tile = 640 if width % 640 == 0 else width
    for d in range(n_tp):
        t = (tp + n_tp - d) % n_tp
        if d > 0:
            attc[d - 1].wait_recv()
        a = att_all[t]
        wrows = pl.ds(pl.multiple_of(t * feats, feats), feats)
        for n in range(width // tile):
            cols = pl.ds(n * tile, tile)
            part = jnp.dot(a, w_in[wrows, cols], preferred_element_type=F32)
            if d == 0:
                part = part + res_in[:, cols].astype(F32)
            else:
                part = part + total_ref[:, cols]
            if d < n_tp - 1:
                total_ref[:, cols] = part
            else:
                out_ref[:, cols] = part.astype(out_ref.dtype)

    for g in gcopies:
        g.wait_send()
    for line in first + last:
        for c in line:
            c.wait_send()
    for m in range(PIECES):
        for d in (0, 1):

            @pl.when(has_target(d))
            def _():
                chain_copy(m, d).wait_send()

    for c in attc:
        c.wait_send()


def body(
    n_req,
    n_tp,
    q_proj,
    kv_proj,
    q_bias,
    kv_bias,
    prefix_kv,
    lengths,
    group_of,
    owner,
    positions,
    residual,
    out_weight,
):
    cap, feats = q_proj.shape[1:]
    total = prefix_kv.shape[1] * 2
    rows = total // (QUAD * PIECES)
    groups = owner.shape[0]
    width = residual.shape[2]
    smem = pl.BlockSpec(memory_space=pltpu.SMEM)
    anym = pl.BlockSpec(memory_space=pl.ANY)
    dma = pltpu.SemaphoreType.DMA

    out = pl.pallas_call(
        functools.partial(kernel, n_req, n_tp, groups),
        out_shape=jax.ShapeDtypeStruct((cap, width), BF16),
        in_specs=[smem] * 4 + [anym] * 7,
        out_specs=pl.BlockSpec(memory_space=pltpu.VMEM),
        scratch_shapes=[
            pltpu.VMEM((cap, feats), BF16),
            pltpu.VMEM((2 * cap, HD), BF16),
            pltpu.VMEM((1, feats), BF16),
            pltpu.VMEM((2, HD), BF16),
            pltpu.VMEM((cap, width), BF16),
            pltpu.VMEM(out_weight.shape, BF16),
            pltpu.VMEM((feats, HD), BF16),
            pltpu.VMEM((max(2 * cap, QUAD * rows), HD), F32),
            pltpu.VMEM((8, 128), jnp.int32),
            pltpu.VMEM((QUAD - 1, 8, 128), jnp.int32),
            pltpu.SMEM((QUAD - 1, 8, 128), jnp.int32),
            pltpu.VMEM((n_tp, cap, feats), BF16),
            pltpu.VMEM((cap, width), F32),
            [pltpu.VMEM((QUAD, rows, HD), BF16)] * PIECES,
            [pltpu.VMEM((2, groups, rows, HD), BF16)] * PIECES,
            [pltpu.VMEM((2, groups, rows, HD), BF16)] * PIECES,
            [pltpu.VMEM((QUAD - 1, rows, HD), BF16)] * PIECES,
            [pltpu.VMEM((QUAD, rows, HD), BF16)] * PIECES,
            dma((7 + PIECES,)),
            dma((PIECES, QUAD - 1)),
            dma((PIECES, QUAD - 1)),
            dma((PIECES, 2)),
            dma((PIECES, 2)),
            dma((PIECES, QUAD - 1)),
            dma((PIECES, QUAD - 1)),
            dma((QUAD - 1,)),
            dma((QUAD - 1,)),
            dma((max(n_tp - 1, 1),)),
            dma((max(n_tp - 1, 1),)),
        ],
        compiler_params=pltpu.CompilerParams(
            collective_id=0, has_side_effects=True, vmem_limit_bytes=60 * 1024 * 1024
        ),
        cost_estimate=pl.CostEstimate(
            flops=2 * cap * out_weight.shape[0] * width + 4 * cap * feats * (total // 2 + cap),
            bytes_accessed=2 * (out_weight.size + 2 * cap * width + total * HD),
            transcendentals=cap * feats // HD * (total // 2 + cap),
        ),
    )(
        lengths,
        group_of,
        owner,
        positions,
        q_proj[0],
        kv_proj[0].reshape(2 * cap, HD),
        q_bias.reshape(1, feats),
        kv_bias,
        prefix_kv[0].reshape(total, HD),
        residual[0],
        out_weight,
    )
    return out[None]


def solution(mesh):
    in_specs = (
        P("req", None, "tp"),
        P("req", None, None, "tp"),
        P("tp"),
        P(None, "tp"),
        P("req", None, None, "tp"),
        P("req"),
        P("req"),
        P(),
        P("req", None),
        P("req", None, "tp"),
        P(None, "tp"),
    )
    out_specs = P("req", None, "tp")
    run = functools.partial(body, mesh.shape["req"], mesh.shape["tp"])
    return jax.shard_map(run, mesh=mesh, in_specs=in_specs, out_specs=out_specs, check_vma=False)
```

time: 150 us -> 67.5 us (0.45)
  waiting for transfers between devices: 119 us -> 0 us
  Pallas kernels: 0 us -> 61.9 us
  between operations: 16.8 us -> 1.31 us
  matrix products: 5.56 us -> 0 us
  other arithmetic: 4.34 us -> 0 us
  blocking collectives: 2.07 us -> 0 us
    psum x1 -> x0, waiting for transfers between devices: 119 us -> none  [spread(): return lax.psum(jnp.where(mine, x, jnp.zeros_like(x)), axis)]
    pallas_call x0 -> x1, Pallas kernels: none -> 61.9 us  [body(): pl.pallas_call(functools.partial(kernel, n_req, n_tp, groups), out_shape=...]
    dot_general x3 -> x0, matrix products: 4.64 us -> none  [the longest x1 3.66 us: body(): jnp.dot(whole_heads, out_weight, preferred_element_type=jnp.float32)]
    select_n x2 -> x0, other arithmetic: 3.43 us -> none  [the longest x1 2.31 us: spread(): return lax.psum(jnp.where(mine, x, jnp.zeros_like(x)), axis)]
    all_gather x1 -> x0, blocking collectives: 2.07 us -> none  [body(): whole_heads = lax.all_gather(attended, 'tp', axis=1, tiled=True)]
    unnamed x13 -> x1, local copies, waits for them, and re-layouts: 0.15 us -> 1.97 us
  transfers between devices with their start and end apart: 1 -> 0, of which waited for: 1 -> 0; matrix products, arithmetic and copies ran while one was open for 1% -> 0% of each run, Pallas kernels for 0% -> 0%
where the time goes in v1:
time: 67.5 us; the launch traced here: 66.4 us
  Pallas kernels  61.9 us (92%)
  local copies, waits for them, and re-layouts  3.21 us (5%)
  between operations  1.31 us (2%)
    pallas_call x1, Pallas kernels, body(): pl.pallas_call(functools.partial(kernel, n_req, n_tp, groups), out_shape=...  61.9 us
    unnamed x1, local copies, waits for them, and re-layouts  1.97 us

profile of v1, /device:TPU:1, one launch (start us, length us, event | category | flops | bytes accessed | tf_op | source)
XLA Modules:
  0.0 66.4 jit_solution(15512353618558643592)
XLA Ops:
  1.3 1.2 %reshape.3.qb_hbm = bf16[1,384]{1,0:T(2,128)(2,1)} reshape(bf16[384]{0:T(512)(128)(2,1)} %param.13) | data formatting | bytes 1536 | tf_op jit(solution)/shard_map/reshape | solution.py:401
  2.5 61.9 %shard_map.109 = bf16[128,2560]{1,0:T(8,128)(2,1)} custom-call(s32[1]{0:T(128)S(6)} %copy.13.length_ref, s32[1]{0:T(128)S(6)} %copy.14.group_ref, s32[3]{0:T(128)} %owner_ref.1, s32[1,128]{1,0:T(1,128)} %pos_ref.1, bf16[128,384]{1,0:T(8,128)(2,1)} %bitcast.8, bf16[256,128]{1,0:T(8,128)(2,1)} %bitcast.9, bf16[1,384]{1,0:T(2,128)(2,1)} %reshape.3.qb_hbm, ...), custom_call_target="tpu_custom_call" | custom-call | flops 729808896 | bytes 5767168 | tf_op jit(solution)/shard_map/pallas_call | solution.py:350
  64.4 2.0 %copy.15 = bf16[1,128,2560]{2,1,0:T(8,128)(2,1)} copy(bf16[1,128,2560]{2,1,0:T(8,128)(2,1)} %bitcast.5) | data formatting | bytes 1310720

commit v2 on v1

--- a/solution.py
+++ b/solution.py
@@ -157,7 +157,7 @@
 
     for h in range(heads):
         cols = pl.ds(h * HD, HD)
-        x = q_in[:, cols].astype(F32) + qb_in[:, cols].astype(F32)
+        x = q_in[:, cols].astype(F32) + qb_in[cols].astype(F32)[None, :]
         queries[pl.ds(h * cap, cap), :] = rot(x).astype(BF16)
     split[pl.ds(0, 2 * cap), :] = kv_in[...].astype(F32)
     bias = kvb_in[...].astype(F32)
@@ -197,32 +197,25 @@
             device_id_type=MESH,
         )
 
-    def has_source(d):
-        return jnp.where(d == 0, k, depth - 1 - k) > 0
-
     def has_target(d):
         return jnp.where(d == 0, depth - 1 - k, k) > 0
 
+    is_end = jnp.logical_or(k == 0, k == depth - 1)
     last = []
 
-    def stage_two(m):
+    def arrive(m):
         for c in first[m]:
             c.wait_recv()
         own[m].wait()
-        for d in (near, 1 - near):
-
-            @pl.when(has_source(d))
-            def _():
-                chain_copy(m, d).wait_recv()
-
-            @pl.when(has_target(d))
-            def _():
-                for c in range(groups):
-                    o = owner_ref[c]
-                    mine = p1[m][o % QUAD]
-                    fwd[m][d, c] = jnp.where(o // QUAD == k, mine, chain[m][d, c])
-                chain_copy(m, d).start()
-
+
+    def forward(m, d):
+        for c in range(groups):
+            o = owner_ref[c]
+            mine = p1[m][o % QUAD]
+            fwd[m][d, c] = jnp.where(o // QUAD == k, mine, chain[m][d, c])
+        chain_copy(m, d).start()
+
+    def hand_out(m):
         line = []
         for d in (1, 2, 3, 0):
             c = wants[d]
@@ -262,10 +255,31 @@
         acc = acc * fade + jnp.dot(w.astype(BF16), vs, preferred_element_type=F32)
         return new, tot, acc
 
-    for m in range(PIECES):
-        stage_two(m)
-        if m > 0:
-            top, tot, acc = attend(m - 1, top, tot, acc)
+    @pl.when(is_end)
+    def _():
+        for m in range(PIECES):
+            arrive(m)
+            forward(m, near)
+
+    for t in range(PIECES + 1):
+        if t < PIECES:
+
+            @pl.when(jnp.logical_not(is_end))
+            def _():
+                arrive(t)
+                chain_copy(t, near).wait_recv()
+                forward(t, near)
+
+        if t > 0:
+            chain_copy(t - 1, 1 - near).wait_recv()
+
+            @pl.when(jnp.logical_not(is_end))
+            def _():
+                forward(t - 1, 1 - near)
+
+            hand_out(t - 1)
+        if t > 1:
+            top, tot, acc = attend(t - 2, top, tot, acc)
     top, tot, acc = attend(PIECES - 1, top, tot, acc)
 
     mixed = acc / tot
@@ -355,7 +369,7 @@
         scratch_shapes=[
             pltpu.VMEM((cap, feats), BF16),
             pltpu.VMEM((2 * cap, HD), BF16),
-            pltpu.VMEM((1, feats), BF16),
+            pltpu.VMEM((feats,), BF16),
             pltpu.VMEM((2, HD), BF16),
             pltpu.VMEM((cap, width), BF16),
             pltpu.VMEM(out_weight.shape, BF16),
@@ -398,7 +412,7 @@
         positions,
         q_proj[0],
         kv_proj[0].reshape(2 * cap, HD),
-        q_bias.reshape(1, feats),
+        q_bias,
         kv_bias,
         prefix_kv[0].reshape(total, HD),
         residual[0],

time: 67.5 us -> 41.9 us (0.62); the launches traced: 66.4 us -> 41.7 us
  Pallas kernels: 61.9 us -> 38.5 us
  local copies, waits for them, and re-layouts: 3.21 us -> 1.97 us
    pallas_call x1, Pallas kernels: 61.9 us -> 38.5 us  [body(): pl.pallas_call(functools.partial(kernel, n_req, n_tp, groups), out_shape=...]
    reshape x1 -> x0, local copies, waits for them, and re-layouts: 1.24 us -> none  [body(): q_bias.reshape(1, feats)]
where the time goes in v2:
time: 41.9 us; the launch traced here: 41.7 us
  Pallas kernels  38.5 us (92%)
  local copies, waits for them, and re-layouts  1.97 us (5%)
  between operations  1.3 us (3%)
    pallas_call x1, Pallas kernels, body(): pl.pallas_call(functools.partial(kernel, n_req, n_tp, groups), out_shape=...  38.5 us
    unnamed x1, local copies, waits for them, and re-layouts  1.97 us

profile of v2, /device:TPU:1, one launch (start us, length us, event | category | flops | bytes accessed | tf_op | source)
XLA Modules:
  0.0 41.7 jit_solution(18255508790392722119)
XLA Ops:
  1.3 38.5 %shard_map.109 = bf16[128,2560]{1,0:T(8,128)(2,1)} custom-call(s32[1]{0:T(128)S(6)} %copy.13.length_ref, s32[1]{0:T(128)S(6)} %copy.14.group_ref, s32[3]{0:T(128)} %owner_ref.1, s32[1,128]{1,0:T(1,128)} %pos_ref.1, bf16[128,384]{1,0:T(8,128)(2,1)} %bitcast.8, bf16[256,128]{1,0:T(8,128)(2,1)} %bitcast.9, bf16[384]{0:T(512)(128)(2,1)} %qb_hbm.1, ...), custom_call_target="tpu_custom_call" | custom-call | flops 729808896 | bytes 5767168 | tf_op jit(solution)/shard_map/pallas_call | solution.py:364
  39.8 2.0 %copy.15 = bf16[1,128,2560]{2,1,0:T(8,128)(2,1)} copy(bf16[1,128,2560]{2,1,0:T(8,128)(2,1)} %bitcast.5) | data formatting | bytes 1310720

commit v3 on v2

--- a/solution.py
+++ b/solution.py
@@ -10,7 +10,7 @@
 
 HD = 128
 QUAD = 4
-PIECES = 4
+PIECES = 8
 MESH = pl.DeviceIdType.MESH
 BF16 = jnp.bfloat16
 F32 = jnp.float32
@@ -40,6 +40,9 @@
     w_in,
     queries,
     split,
+    top_ref,
+    tot_ref,
+    acc_ref,
     gsend,
     grecv,
     gsmem,
@@ -141,6 +144,41 @@
     for f in fetches[4:]:
         f.start()
 
+    near = jnp.where(k < depth // 2, 0, 1)
+
+    def chain_copy(m, d):
+        step = 1 - 2 * d
+        return pltpu.make_async_remote_copy(
+            src_ref=fwd[m].at[d],
+            dst_ref=chain[m].at[d],
+            send_sem=ch_send.at[m, d],
+            recv_sem=ch_recv.at[m, d],
+            device_id=(req + step * QUAD, tp),
+            device_id_type=MESH,
+        )
+
+    def has_target(d):
+        return jnp.where(d == 0, depth - 1 - k, k) > 0
+
+    is_end = jnp.logical_or(k == 0, k == depth - 1)
+    def arrive(m):
+        for c in first[m]:
+            c.wait_recv()
+        own[m].wait()
+
+    def forward(m, d):
+        for c in range(groups):
+            o = owner_ref[c]
+            mine = p1[m][o % QUAD]
+            fwd[m][d, c] = jnp.where(o // QUAD == k, mine, chain[m][d, c])
+        chain_copy(m, d).start()
+
+    @pl.when(is_end)
+    def _():
+        for m in range(PIECES):
+            arrive(m)
+            forward(m, near)
+
     for f in fetches[:4]:
         f.wait()
     lane = lax.broadcasted_iota(jnp.int32, (cap, HD), 1)
@@ -172,8 +210,9 @@
     s = jnp.where(seen, s, -1e30)
     top = jnp.max(s, axis=-1, keepdims=True)
     w = jnp.where(seen, jnp.exp(s - top), 0.0)
-    tot = jnp.sum(w, axis=-1, keepdims=True)
-    acc = jnp.dot(w.astype(BF16), vals, preferred_element_type=F32)
+    top_ref[...] = top
+    tot_ref[...] = jnp.sum(w, axis=-1, keepdims=True)
+    acc_ref[...] = jnp.dot(w.astype(BF16), vals, preferred_element_type=F32)
 
     for d in range(1, QUAD):
         gcopies[d - 1].wait_recv()
@@ -184,36 +223,7 @@
     for d in range(1, QUAD):
         wants.append(gsmem[QUAD - d - 1, 0, 0])
 
-    near = jnp.where(k < depth // 2, 0, 1)
-
-    def chain_copy(m, d):
-        step = 1 - 2 * d
-        return pltpu.make_async_remote_copy(
-            src_ref=fwd[m].at[d],
-            dst_ref=chain[m].at[d],
-            send_sem=ch_send.at[m, d],
-            recv_sem=ch_recv.at[m, d],
-            device_id=(req + step * QUAD, tp),
-            device_id_type=MESH,
-        )
-
-    def has_target(d):
-        return jnp.where(d == 0, depth - 1 - k, k) > 0
-
-    is_end = jnp.logical_or(k == 0, k == depth - 1)
     last = []
-
-    def arrive(m):
-        for c in first[m]:
-            c.wait_recv()
-        own[m].wait()
-
-    def forward(m, d):
-        for c in range(groups):
-            o = owner_ref[c]
-            mine = p1[m][o % QUAD]
-            fwd[m][d, c] = jnp.where(o // QUAD == k, mine, chain[m][d, c])
-        chain_copy(m, d).start()
 
     def hand_out(m):
         line = []
@@ -239,28 +249,27 @@
                 line.append(r)
         last.append(line)
 
-    def attend(m, top, tot, acc):
-        for r in last[m]:
-            r.wait_recv()
-        for j in range(QUAD):
-            split[pl.ds(j * rows, rows), :] = kvp[m][j].astype(F32)
-        half = QUAD * rows // 2
+    def attend(pieces):
+        span = QUAD * rows
+        for i, m in enumerate(pieces):
+            for r in last[m]:
+                r.wait_recv()
+            for j in range(QUAD):
+                split[pl.ds(i * span + j * rows, rows), :] = kvp[m][j].astype(F32)
+        half = len(pieces) * span // 2
         ks = split[pl.ds(0, half, stride=2), :].astype(BF16)
         vs = split[pl.ds(1, half, stride=2), :].astype(BF16)
         s = lax.dot_general(queries[...], ks, nt, preferred_element_type=F32) * scale
+        top = top_ref[...]
         new = jnp.maximum(top, jnp.max(s, axis=-1, keepdims=True))
         fade = jnp.exp(top - new)
         w = jnp.exp(s - new)
-        tot = tot * fade + jnp.sum(w, axis=-1, keepdims=True)
-        acc = acc * fade + jnp.dot(w.astype(BF16), vs, preferred_element_type=F32)
-        return new, tot, acc
-
-    @pl.when(is_end)
-    def _():
-        for m in range(PIECES):
-            arrive(m)
-            forward(m, near)
-
+        top_ref[...] = new
+        tot_ref[...] = tot_ref[...] * fade + jnp.sum(w, axis=-1, keepdims=True)
+        acc_ref[...] = acc_ref[...] * fade + jnp.dot(w.astype(BF16), vs, preferred_element_type=F32)
+
+    early = {t: [t - 3, t - 2] for t in range(3, PIECES, 2)}
+    early[PIECES] = [PIECES - 2]
     for t in range(PIECES + 1):
         if t < PIECES:
 
@@ -278,11 +287,22 @@
                 forward(t - 1, 1 - near)
 
             hand_out(t - 1)
-        if t > 1:
-            top, tot, acc = attend(t - 2, top, tot, acc)
-    top, tot, acc = attend(PIECES - 1, top, tot, acc)
-
-    mixed = acc / tot
+        if t in early:
+
+            @pl.when(is_end)
+            def _():
+                attend(early[t])
+
+    @pl.when(is_end)
+    def _():
+        attend([PIECES - 1])
+
+    @pl.when(jnp.logical_not(is_end))
+    def _():
+        for m in range(0, PIECES, 4):
+            attend(range(m, m + 4))
+
+    mixed = acc_ref[...] / tot_ref[...]
     slot = lax.broadcasted_iota(jnp.int32, mixed.shape, 0) % cap
     mixed = jnp.where(slot < length_ref[0], mixed, 0.0).astype(BF16)
     for h in range(heads):
@@ -374,7 +394,10 @@
             pltpu.VMEM((cap, width), BF16),
             pltpu.VMEM(out_weight.shape, BF16),
             pltpu.VMEM((feats, HD), BF16),
-            pltpu.VMEM((max(2 * cap, QUAD * rows), HD), F32),
+            pltpu.VMEM((max(2 * cap, 4 * QUAD * rows), HD), F32),
+            pltpu.VMEM((feats, 1), F32),
+            pltpu.VMEM((feats, 1), F32),
+            pltpu.VMEM((feats, HD), F32),
             pltpu.VMEM((8, 128), jnp.int32),
             pltpu.VMEM((QUAD - 1, 8, 128), jnp.int32),
             pltpu.SMEM((QUAD - 1, 8, 128), jnp.int32),

time: 41.9 us -> 44.1 us (1.053)
  Pallas kernels: 38.5 us -> 40.6 us
    pallas_call x1, Pallas kernels: 38.5 us -> 40.6 us  [body(): pl.pallas_call(functools.partial(kernel, n_req, n_tp, groups), out_shape=...]
where the time goes in v3:
time: 44.1 us; the launch traced here: 43.9 us
  Pallas kernels  40.6 us (92%)
  local copies, waits for them, and re-layouts  1.97 us (4%)
  between operations  1.3 us (3%)
    pallas_call x1, Pallas kernels, body(): pl.pallas_call(functools.partial(kernel, n_req, n_tp, groups), out_shape=...  40.6 us
    unnamed x1, local copies, waits for them, and re-layouts  1.97 us

profile of v3, /device:TPU:1, one launch (start us, length us, event | category | flops | bytes accessed | tf_op | source)
XLA Modules:
  0.0 43.9 jit_solution(15972535541841221170)
XLA Ops:
  1.3 40.6 %shard_map.109 = bf16[128,2560]{1,0:T(8,128)(2,1)} custom-call(s32[1]{0:T(128)S(6)} %copy.13.length_ref, s32[1]{0:T(128)S(6)} %copy.14.group_ref, s32[3]{0:T(128)} %owner_ref.1, s32[1,128]{1,0:T(1,128)} %pos_ref.1, bf16[128,384]{1,0:T(8,128)(2,1)} %bitcast.8, bf16[256,128]{1,0:T(8,128)(2,1)} %bitcast.9, bf16[384]{0:T(512)(128)(2,1)} %qb_hbm.1, ...), custom_call_target="tpu_custom_call" | custom-call | flops 729808896 | bytes 5767168 | tf_op jit(solution)/shard_map/pallas_call | solution.py:384
  41.9 2.0 %copy.15 = bf16[1,128,2560]{2,1,0:T(8,128)(2,1)} copy(bf16[1,128,2560]{2,1,0:T(8,128)(2,1)} %bitcast.5) | data formatting | bytes 1310720

commit v4 on v3

--- a/solution.py
+++ b/solution.py
@@ -10,7 +10,7 @@
 
 HD = 128
 QUAD = 4
-PIECES = 8
+PIECES = 4
 MESH = pl.DeviceIdType.MESH
 BF16 = jnp.bfloat16
 F32 = jnp.float32
@@ -29,15 +29,11 @@
     qb_hbm,
     kvb_hbm,
     slab_hbm,
-    res_hbm,
-    w_hbm,
-    out_ref,
+    att_all,
     q_in,
     kv_in,
     qb_in,
     kvb_in,
-    res_in,
-    w_in,
     queries,
     split,
     top_ref,
@@ -46,8 +42,6 @@
     gsend,
     grecv,
     gsmem,
-    att_all,
-    total_ref,
     p1,
     chain,
     fwd,
@@ -81,10 +75,10 @@
 
     fetches = []
     for i, (src, dst) in enumerate(
-        ((q_hbm, q_in), (kv_hbm, kv_in), (qb_hbm, qb_in), (kvb_hbm, kvb_in), (res_hbm, res_in), (w_hbm, w_in))
+        ((q_hbm, q_in), (kv_hbm, kv_in), (qb_hbm, qb_in), (kvb_hbm, kvb_in))
     ):
         fetches.append(pltpu.make_async_copy(src, dst, local_sem.at[i]))
-    for f in fetches[:4]:
+    for f in fetches:
         f.start()
 
     barrier = pltpu.get_barrier_semaphore()
@@ -131,18 +125,21 @@
                 device_id=(mate(d), tp),
                 device_id_type=MESH,
             )
-            c.start()
             line.append(c)
         start = pl.multiple_of((q * PIECES + m) * rows, rows)
         c = pltpu.make_async_copy(slab_hbm.at[pl.ds(start, rows)], p1[m].at[q], local_sem.at[6 + m])
-        c.start()
         own.append(c)
         first.append(line)
-        if m == 0:
-            for g in gcopies:
-                g.start()
-    for f in fetches[4:]:
-        f.start()
+
+    def depart(m):
+        if m < PIECES:
+            for c in first[m] + [own[m]]:
+                c.start()
+
+    depart(0)
+    for g in gcopies:
+        g.start()
+    depart(1)
 
     near = jnp.where(k < depth // 2, 0, 1)
 
@@ -177,9 +174,10 @@
     def _():
         for m in range(PIECES):
             arrive(m)
+            depart(m + 2)
             forward(m, near)
 
-    for f in fetches[:4]:
+    for f in fetches:
         f.wait()
     lane = lax.broadcasted_iota(jnp.int32, (cap, HD), 1)
     place = (pos_ref[0, 0] + lax.broadcasted_iota(jnp.int32, (cap, HD), 0)).astype(F32)
@@ -268,14 +266,14 @@
         tot_ref[...] = tot_ref[...] * fade + jnp.sum(w, axis=-1, keepdims=True)
         acc_ref[...] = acc_ref[...] * fade + jnp.dot(w.astype(BF16), vs, preferred_element_type=F32)
 
-    early = {t: [t - 3, t - 2] for t in range(3, PIECES, 2)}
-    early[PIECES] = [PIECES - 2]
+    early = {t: [t - 2] for t in range(2, PIECES + 1)}
     for t in range(PIECES + 1):
         if t < PIECES:
 
             @pl.when(jnp.logical_not(is_end))
             def _():
                 arrive(t)
+                depart(t + 2)
                 chain_copy(t, near).wait_recv()
                 forward(t, near)
 
@@ -299,8 +297,8 @@
 
     @pl.when(jnp.logical_not(is_end))
     def _():
-        for m in range(0, PIECES, 4):
-            attend(range(m, m + 4))
+        for m in range(0, PIECES, 2):
+            attend(range(m, m + 2))
 
     mixed = acc_ref[...] / tot_ref[...]
     slot = lax.broadcasted_iota(jnp.int32, mixed.shape, 0) % cap
@@ -319,27 +317,8 @@
         )
         c.start()
         attc.append(c)
-    for f in fetches[4:]:
-        f.wait()
-    width = out_ref.shape[1]
-    tile = 640 if width % 640 == 0 else width
-    for d in range(n_tp):
-        t = (tp + n_tp - d) % n_tp
-        if d > 0:
-            attc[d - 1].wait_recv()
-        a = att_all[t]
-        wrows = pl.ds(pl.multiple_of(t * feats, feats), feats)
-        for n in range(width // tile):
-            cols = pl.ds(n * tile, tile)
-            part = jnp.dot(a, w_in[wrows, cols], preferred_element_type=F32)
-            if d == 0:
-                part = part + res_in[:, cols].astype(F32)
-            else:
-                part = part + total_ref[:, cols]
-            if d < n_tp - 1:
-                total_ref[:, cols] = part
-            else:
-                out_ref[:, cols] = part.astype(out_ref.dtype)
+    for c in attc:
+        c.wait_recv()
 
     for g in gcopies:
         g.wait_send()
@@ -355,6 +334,14 @@
 
     for c in attc:
         c.wait_send()
+
+
+def project(n_tp, att_ref, w_ref, res_ref, out_ref):
+    feats = att_ref.shape[2]
+    total = res_ref[...].astype(F32)
+    for t in range(n_tp):
+        total = total + jnp.dot(att_ref[t], w_ref[pl.ds(t * feats, feats), :], preferred_element_type=F32)
+    out_ref[...] = total.astype(BF16)
 
 
 def body(
@@ -381,28 +368,24 @@
     anym = pl.BlockSpec(memory_space=pl.ANY)
     dma = pltpu.SemaphoreType.DMA
 
-    out = pl.pallas_call(
+    att = pl.pallas_call(
         functools.partial(kernel, n_req, n_tp, groups),
-        out_shape=jax.ShapeDtypeStruct((cap, width), BF16),
-        in_specs=[smem] * 4 + [anym] * 7,
+        out_shape=jax.ShapeDtypeStruct((n_tp, cap, feats), BF16),
+        in_specs=[smem] * 4 + [anym] * 5,
         out_specs=pl.BlockSpec(memory_space=pltpu.VMEM),
         scratch_shapes=[
             pltpu.VMEM((cap, feats), BF16),
             pltpu.VMEM((2 * cap, HD), BF16),
             pltpu.VMEM((feats,), BF16),
             pltpu.VMEM((2, HD), BF16),
-            pltpu.VMEM((cap, width), BF16),
-            pltpu.VMEM(out_weight.shape, BF16),
             pltpu.VMEM((feats, HD), BF16),
-            pltpu.VMEM((max(2 * cap, 4 * QUAD * rows), HD), F32),
+            pltpu.VMEM((max(2 * cap, 2 * QUAD * rows), HD), F32),
             pltpu.VMEM((feats, 1), F32),
             pltpu.VMEM((feats, 1), F32),
             pltpu.VMEM((feats, HD), F32),
             pltpu.VMEM((8, 128), jnp.int32),
             pltpu.VMEM((QUAD - 1, 8, 128), jnp.int32),
             pltpu.SMEM((QUAD - 1, 8, 128), jnp.int32),
-            pltpu.VMEM((n_tp, cap, feats), BF16),
-            pltpu.VMEM((cap, width), F32),
             [pltpu.VMEM((QUAD, rows, HD), BF16)] * PIECES,
             [pltpu.VMEM((2, groups, rows, HD), BF16)] * PIECES,
             [pltpu.VMEM((2, groups, rows, HD), BF16)] * PIECES,
@@ -424,8 +407,8 @@
             collective_id=0, has_side_effects=True, vmem_limit_bytes=60 * 1024 * 1024
         ),
         cost_estimate=pl.CostEstimate(
-            flops=2 * cap * out_weight.shape[0] * width + 4 * cap * feats * (total // 2 + cap),
-            bytes_accessed=2 * (out_weight.size + 2 * cap * width + total * HD),
+            flops=4 * cap * feats * (total // 2 + cap),
+            bytes_accessed=4 * total * HD,
             transcendentals=cap * feats // HD * (total // 2 + cap),
         ),
     )(
@@ -438,9 +421,25 @@
         q_bias,
         kv_bias,
         prefix_kv[0].reshape(total, HD),
-        residual[0],
-        out_weight,
     )
+    tile = 640 if width % 640 == 0 else width
+    out = pl.pallas_call(
+        functools.partial(project, n_tp),
+        grid=(width // tile,),
+        out_shape=jax.ShapeDtypeStruct((cap, width), BF16),
+        in_specs=[
+            pl.BlockSpec((n_tp, cap, feats), lambda n: (0, 0, 0)),
+            pl.BlockSpec((n_tp * feats, tile), lambda n: (0, n)),
+            pl.BlockSpec((cap, tile), lambda n: (0, n)),
+        ],
+        out_specs=pl.BlockSpec((cap, tile), lambda n: (0, n)),
+        compiler_params=pltpu.CompilerParams(vmem_limit_bytes=60 * 1024 * 1024),
+        cost_estimate=pl.CostEstimate(
+            flops=2 * cap * out_weight.shape[0] * width,
+            bytes_accessed=2 * (out_weight.size + 2 * cap * width),
+            transcendentals=0,
+        ),
+    )(att, out_weight, residual[0])
     return out[None]
 
 

time: 44.1 us -> 43.3 us (0.982)
  local copies, waits for them, and re-layouts: 1.97 us -> 0 us
  Pallas kernels: 40.6 us -> 41.8 us
    pallas_call x0 -> x1, Pallas kernels: none -> 4.69 us  [body(): pl.pallas_call(functools.partial(project, n_tp), grid=(width // tile,), o...]
    pallas_call x1, Pallas kernels: 40.6 us -> 37.1 us  [body(): pl.pallas_call(functools.partial(kernel, n_req, n_tp, groups), out_shape=...]
    unnamed x1 -> x0, local copies, waits for them, and re-layouts: 1.97 us -> none
where the time goes in v4:
time: 43.3 us; the launch traced here: 43.1 us
  Pallas kernels  41.8 us (97%)
  between operations  1.3 us (3%)
    pallas_call x1, Pallas kernels, body(): pl.pallas_call(functools.partial(kernel, n_req, n_tp, groups), out_shape=...  37.1 us
    pallas_call x1, Pallas kernels, body(): pl.pallas_call(functools.partial(project, n_tp), grid=(width // tile,), o...  4.69 us

profile of v4, /device:TPU:1, one launch (start us, length us, event | category | flops | bytes accessed | tf_op | source)
XLA Modules:
  0.0 43.1 jit_solution(2313069176485262554)
XLA Ops:
  1.3 37.1 %shard_map.109.att_ref = bf16[2,128,384]{2,1,0:T(8,128)(2,1)} custom-call(s32[1]{0:T(128)S(6)} %copy.12.length_ref, s32[1]{0:T(128)S(6)} %copy.13.group_ref, s32[3]{0:T(128)} %owner_ref.1, s32[1,128]{1,0:T(1,128)} %pos_ref.1, bf16[128,384]{1,0:T(8,128)(2,1)} %bitcast.7, bf16[256,128]{1,0:T(8,128)(2,1)} %bitcast.8, bf16[384]{0:T(512)(128)(2,1)} %qb_hbm.1, ...), custom_call_target="tpu_custom_call" | custom-call | flops 226492416 | bytes 1048576 | tf_op jit(solution)/shard_map/pallas_call | solution.py:371
  38.4 4.7 %shard_map.110 = bf16[128,2560]{1,0:T(8,128)(2,1)} custom-call(bf16[2,128,384]{2,1,0:T(8,128)(2,1)} %shard_map.109.att_ref, bf16[768,2560]{1,0:T(8,128)(2,1)} %w_ref.1, bf16[128,2560]{1,0:T(8,128)(2,1)} %bitcast.5), custom_call_target="tpu_custom_call" | custom-call | flops 503316480 | bytes 5242880 | tf_op jit(solution)/shard_map/pallas_call | solution.py:426

commit v5 on v3

--- a/solution.py
+++ b/solution.py
@@ -10,7 +10,7 @@
 
 HD = 128
 QUAD = 4
-PIECES = 8
+PIECES = 4
 MESH = pl.DeviceIdType.MESH
 BF16 = jnp.bfloat16
 F32 = jnp.float32
@@ -131,28 +131,33 @@
                 device_id=(mate(d), tp),
                 device_id_type=MESH,
             )
-            c.start()
             line.append(c)
         start = pl.multiple_of((q * PIECES + m) * rows, rows)
         c = pltpu.make_async_copy(slab_hbm.at[pl.ds(start, rows)], p1[m].at[q], local_sem.at[6 + m])
-        c.start()
         own.append(c)
         first.append(line)
-        if m == 0:
-            for g in gcopies:
-                g.start()
+
+    def depart(m):
+        if m < PIECES:
+            for c in first[m] + [own[m]]:
+                c.start()
+
+    depart(0)
+    for g in gcopies:
+        g.start()
+    depart(1)
     for f in fetches[4:]:
         f.start()
 
     near = jnp.where(k < depth // 2, 0, 1)
 
-    def chain_copy(m, d):
+    def chain_copy(m, d, c):
         step = 1 - 2 * d
         return pltpu.make_async_remote_copy(
-            src_ref=fwd[m].at[d],
-            dst_ref=chain[m].at[d],
-            send_sem=ch_send.at[m, d],
-            recv_sem=ch_recv.at[m, d],
+            src_ref=fwd[m].at[d, c],
+            dst_ref=chain[m].at[d, c],
+            send_sem=ch_send.at[m, d * groups + c],
+            recv_sem=ch_recv.at[m, d * groups + c],
             device_id=(req + step * QUAD, tp),
             device_id_type=MESH,
         )
@@ -166,18 +171,26 @@
             c.wait_recv()
         own[m].wait()
 
-    def forward(m, d):
+    def forward(m, d, wait):
         for c in range(groups):
+            if wait:
+                chain_copy(m, d, c).wait_recv()
             o = owner_ref[c]
             mine = p1[m][o % QUAD]
             fwd[m][d, c] = jnp.where(o // QUAD == k, mine, chain[m][d, c])
-        chain_copy(m, d).start()
+            chain_copy(m, d, c).start()
 
     @pl.when(is_end)
     def _():
         for m in range(PIECES):
             arrive(m)
-            forward(m, near)
+            depart(m + 2)
+            forward(m, near, False)
+
+    @pl.when(jnp.logical_not(is_end))
+    def _():
+        for m in range(2, PIECES):
+            depart(m)
 
     for f in fetches[:4]:
         f.wait()
@@ -268,23 +281,25 @@
         tot_ref[...] = tot_ref[...] * fade + jnp.sum(w, axis=-1, keepdims=True)
         acc_ref[...] = acc_ref[...] * fade + jnp.dot(w.astype(BF16), vs, preferred_element_type=F32)
 
-    early = {t: [t - 3, t - 2] for t in range(3, PIECES, 2)}
-    early[PIECES] = [PIECES - 2]
+    early = {t: [t - 2] for t in range(2, PIECES + 1)}
     for t in range(PIECES + 1):
         if t < PIECES:
 
             @pl.when(jnp.logical_not(is_end))
             def _():
                 arrive(t)
-                chain_copy(t, near).wait_recv()
-                forward(t, near)
+                forward(t, near, True)
 
         if t > 0:
-            chain_copy(t - 1, 1 - near).wait_recv()
+
+            @pl.when(is_end)
+            def _():
+                for c in range(groups):
+                    chain_copy(t - 1, 1 - near, c).wait_recv()
 
             @pl.when(jnp.logical_not(is_end))
             def _():
-                forward(t - 1, 1 - near)
+                forward(t - 1, 1 - near, True)
 
             hand_out(t - 1)
         if t in early:
@@ -299,8 +314,8 @@
 
     @pl.when(jnp.logical_not(is_end))
     def _():
-        for m in range(0, PIECES, 4):
-            attend(range(m, m + 4))
+        for m in range(0, PIECES, 2):
+            attend(range(m, m + 2))
 
     mixed = acc_ref[...] / tot_ref[...]
     slot = lax.broadcasted_iota(jnp.int32, mixed.shape, 0) % cap
@@ -351,7 +366,8 @@
 
             @pl.when(has_target(d))
             def _():
-                chain_copy(m, d).wait_send()
+                for c in range(groups):
+                    chain_copy(m, d, c).wait_send()
 
     for c in attc:
         c.wait_send()
@@ -394,7 +410,7 @@
             pltpu.VMEM((cap, width), BF16),
             pltpu.VMEM(out_weight.shape, BF16),
             pltpu.VMEM((feats, HD), BF16),
-            pltpu.VMEM((max(2 * cap, 4 * QUAD * rows), HD), F32),
+            pltpu.VMEM((max(2 * cap, 2 * QUAD * rows), HD), F32),
             pltpu.VMEM((feats, 1), F32),
             pltpu.VMEM((feats, 1), F32),
             pltpu.VMEM((feats, HD), F32),
@@ -411,8 +427,8 @@
             dma((7 + PIECES,)),
             dma((PIECES, QUAD - 1)),
             dma((PIECES, QUAD - 1)),
-            dma((PIECES, 2)),
-            dma((PIECES, 2)),
+            dma((PIECES, 2 * groups)),
+            dma((PIECES, 2 * groups)),
             dma((PIECES, QUAD - 1)),
             dma((PIECES, QUAD - 1)),
             dma((QUAD - 1,)),

time: 44.1 us -> 38.5 us (0.87)
  Pallas kernels: 40.6 us -> 35 us
    pallas_call x1, Pallas kernels: 40.6 us -> 35 us  [body(): pl.pallas_call(functools.partial(kernel, n_req, n_tp, groups), out_shape=...]
where the time goes in v5:
time: 38.5 us; the launch traced here: 38.3 us
  Pallas kernels  35 us (91%)
  local copies, waits for them, and re-layouts  1.97 us (5%)
  between operations  1.3 us (3%)
    pallas_call x1, Pallas kernels, body(): pl.pallas_call(functools.partial(kernel, n_req, n_tp, groups), out_shape=...  35 us
    unnamed x1, local copies, waits for them, and re-layouts  1.97 us

profile of v5, /device:TPU:1, one launch (start us, length us, event | category | flops | bytes accessed | tf_op | source)
XLA Modules:
  0.0 38.3 jit_solution(12365201644749579655)
XLA Ops:
  1.3 35.0 %shard_map.109 = bf16[128,2560]{1,0:T(8,128)(2,1)} custom-call(s32[1]{0:T(128)S(6)} %copy.13.length_ref, s32[1]{0:T(128)S(6)} %copy.14.group_ref, s32[3]{0:T(128)} %owner_ref.1, s32[1,128]{1,0:T(1,128)} %pos_ref.1, bf16[128,384]{1,0:T(8,128)(2,1)} %bitcast.8, bf16[256,128]{1,0:T(8,128)(2,1)} %bitcast.9, bf16[384]{0:T(512)(128)(2,1)} %qb_hbm.1, ...), custom_call_target="tpu_custom_call" | custom-call | flops 729808896 | bytes 5767168 | tf_op jit(solution)/shard_map/pallas_call | solution.py:400
  36.3 2.0 %copy.15 = bf16[1,128,2560]{2,1,0:T(8,128)(2,1)} copy(bf16[1,128,2560]{2,1,0:T(8,128)(2,1)} %bitcast.5) | data formatting | bytes 1310720
